TPU v7x, 512 devices: a whole 4x4x16 slice. The times are simulated.
512 devices in a mesh: blk: 16 (over z), uly: 8 (over x, y_hi), clip: 4 (over y_lo, core).
Axes of the slice: x: 4, y: 4 (y_hi: 2, y_lo: 2; y = y_hi * 2 + y_lo), z: 16, core: 2. Of those that a mesh axis runs over, the one named last changes fastest.
Arguments:
- self_queries: bfloat16 [16384, 3072], P(('clip', 'blk', 'uly')), parts along dimension 0, may hold values from -160 to 160
- self_keys: bfloat16 [16384, 3072], P(('clip', 'blk', 'uly')), parts along dimension 0, may hold values from -6 to 6
- self_values: bfloat16 [16384, 3072], P(('clip', 'blk', 'uly')), parts along dimension 0, may hold values from -6 to 6
- cross_queries: bfloat16 [16384, 3072], P(('clip', 'blk', 'uly')), parts along dimension 0, may hold values from -160 to 160
- text_rows: bfloat16 [1024, 4096], P('clip'), parts along dimension 0, may hold values from -6 to 6
- text_projection: bfloat16 [4096, 2, 3072], P('blk', None, 'uly'), may hold values from -0.09375 to 0.09375
Outputs:
- attended: bfloat16 [16384, 3072], P(('clip', 'blk', 'uly')), parts along dimension 0
There are 4 independent parts, one for each index of `clip`. A program takes and returns all parts, laid end to end along the dimension named above; an argument that names none is the same for every part. Nothing has to cross between parts.
All inputs are finite; a program needn't handle non-finite values.
Results may differ from a plain program's by a relative error of at most 0.012.
Values may be sent and summed in bfloat16 or wider, within the bound.
A program may use at most 128 MiB of HBM per device.

v0:
```python
import jax
import jax.numpy as jnp
from jax import lax
from jax.sharding import PartitionSpec as P

HEAD_DIM = 128


def on_device(self_queries, self_keys, self_values, cross_queries, text_rows, text_projection):
    regrouped = (
        lax.all_to_all(self_queries, "uly", split_axis=1, concat_axis=0, tiled=True),
        lax.all_to_all(self_keys, "uly", split_axis=1, concat_axis=0, tiled=True),
        lax.all_to_all(self_values, "uly", split_axis=1, concat_axis=0, tiled=True),
        lax.all_to_all(cross_queries, "uly", split_axis=1, concat_axis=0, tiled=True),
    )
    local_query, local_key, local_value, local_cross = regrouped
    row_count = local_query.shape[0]
    head_count = local_query.shape[1] // HEAD_DIM
    score_scale = HEAD_DIM ** (-0.5)
    query_heads = local_query.reshape(row_count, head_count, HEAD_DIM)
    start_top = jnp.full((head_count, row_count), -jnp.inf, jnp.float32)
    start_total = jnp.zeros((head_count, row_count), jnp.float32)
    start_acc = jnp.zeros((head_count, row_count, HEAD_DIM), jnp.float32)
    key_block = lax.all_gather(local_key, "blk", axis=0, tiled=True)
    value_block = lax.all_gather(local_value, "blk", axis=0, tiled=True)
    block_len = key_block.shape[0]
    key_heads = key_block.reshape(block_len, head_count, HEAD_DIM)
    value_heads = value_block.reshape(block_len, head_count, HEAD_DIM)
    scores = (
        jnp.einsum("rhd,nhd->hrn", query_heads, key_heads, preferred_element_type=jnp.float32)
        * score_scale
    )
    new_top = jnp.max(scores, axis=-1)
    shrink = jnp.exp(start_top - new_top)
    weights = jnp.exp(scores - new_top[..., None])
    new_total = start_total * shrink + jnp.sum(weights, axis=-1)
    update = jnp.einsum(
        "hrn,nhd->hrd",
        weights.astype(jnp.bfloat16),
        value_heads,
        preferred_element_type=jnp.float32,
    )
    final_acc = start_acc * shrink[..., None] + update
    self_out = final_acc / new_total[..., None]
    text_count = text_rows.shape[0]
    offset_here = lax.axis_index("blk") * text_projection.shape[0]
    columns = lax.dynamic_slice_in_dim(text_rows, offset_here, text_projection.shape[0], 1)
    projected = lax.psum(
        jnp.einsum("rc,cjk->rjk", columns, text_projection, preferred_element_type=jnp.float32),
        "blk",
    )
    text_kv = projected.astype(jnp.bfloat16)
    text_keys = text_kv[:, 0].reshape(text_count, head_count, HEAD_DIM)
    text_vals = text_kv[:, 1].reshape(text_count, head_count, HEAD_DIM)
    cross_heads = local_cross.reshape(row_count, head_count, HEAD_DIM)
    cross_scores = (
        jnp.einsum("rhd,nhd->hrn", cross_heads, text_keys, preferred_element_type=jnp.float32)
        * score_scale
    )
    cross_top = jnp.max(cross_scores, axis=-1, keepdims=True)
    cross_weights = jnp.exp(cross_scores - cross_top)
    cross_total = jnp.sum(cross_weights, axis=-1)
    cross_out = (
        jnp.einsum(
            "hrn,nhd->hrd",
            cross_weights.astype(jnp.bfloat16),
            text_vals,
            preferred_element_type=jnp.float32,
        )
        / cross_total[..., None]
    )
    combined = (self_out + cross_out).transpose(1, 0, 2).reshape(row_count, head_count * HEAD_DIM)
    combined = combined.astype(jnp.bfloat16)
    return lax.all_to_all(combined, "uly", split_axis=0, concat_axis=1, tiled=True)


def solution(mesh):
    return jax.shard_map(
        on_device,
        mesh=mesh,
        in_specs=(
            P(("clip", "blk", "uly"), None),
            P(("clip", "blk", "uly"), None),
            P(("clip", "blk", "uly"), None),
            P(("clip", "blk", "uly"), None),
            P("clip", None),
            P("blk", None, "uly"),
        ),
        out_specs=P(("clip", "blk", "uly"), None),
        check_vma=False,
    )
```

profile of v0, /device:TPU:32, one launch (start us, length us, event | category | flops | bytes accessed | tf_op | source)
XLA Modules:
  0.0 213.3 jit_solution(4839631090326363835)
XLA Ops:
  6.5 0.0 copy-start
  6.5 0.0 all-gather.3.cloned.1.call-start
  6.5 1.1 copy.88
  7.6 15.0 %all_to_all.86 = bf16[32,8,384]{2,0,1:T(8,128)(2,1)} all-to-all(bf16[32,8,384]{2,0,1:T(8,128)(2,1)S(1)} %bitcast.69), channel_id=1, replica_groups=mesh['blk'=16,'uly'=8,'clip'=4] {'uly'}, dimensions={1} | all-to-all | bytes 393216 | tf_op jit(solution)/shard_map/all_to_all | solution.py:12
  22.6 0.0 all-gather.3.cloned.1.call-update
  22.7 0.0 all-gather.5.cloned.1.call-start
  22.7 0.9 copy.87
  23.7 11.2 %all_to_all.87 = bf16[32,8,384]{2,0,1:T(8,128)(2,1)} all-to-all(bf16[32,8,384]{2,0,1:T(8,128)(2,1)S(1)} %bitcast.70), channel_id=1, replica_groups=mesh['blk'=16,'uly'=8,'clip'=4] {'uly'}, dimensions={1} | all-to-all | bytes 393216 | tf_op jit(solution)/shard_map/all_to_all | solution.py:13
  34.9 0.0 all-gather.5.cloned.1.call-update
  34.9 1.6 copy.89
  36.6 3.4 %all-to-all-start = ((bf16[32,8,384]{2,0,1:T(8,128)(2,1)}), bf16[32,8,384]{2,0,1:T(8,128)(2,1)S(1)}, u32[]{:S(2)}, u32[]{:S(2)}) async-start(bf16[32,8,384]{2,0,1:T(8,128)(2,1)} %bitcast.60), calls=%async_computation | async-start | bytes 393216 | tf_op jit(solution)/shard_map/all_to_all | solution.py:11
  40.0 0.0 copy-done
  40.0 1.3 fusion.22
  41.2 76.2 %all-reduce.1 = bf16[256,2,384]{2,0,1:T(8,128)(2,1)S(1)} all-reduce(f32[256,2,384]{2,0,1:T(8,128)S(1)} %fusion.22), channel_id=1, replica_groups=mesh['blk'=16,'uly'=8,'clip'=4] {'blk'}, use_global_device_ids=true, to_apply=%region_2.0 | all-reduce | flops 196608 | bytes 1179648 | tf_op jit(solution)/shard_map/psum | solution.py:48
  117.4 1.6 copy.86
  119.0 0.0 all-to-all-done
  119.0 7.0 %all-to-all-start.3 = ((bf16[32,8,384]{2,0,1:T(8,128)(2,1)}), bf16[32,8,384]{2,0,1:T(8,128)(2,1)S(1)}, u32[]{:S(2)}, u32[]{:S(2)}) async-start(bf16[32,8,384]{2,0,1:T(8,128)(2,1)} %bitcast.57), calls=%async_computation.3 | async-start | bytes 393216 | tf_op jit(solution)/shard_map/all_to_all | solution.py:14
  126.0 0.8 copy.53
  126.9 0.8 copy.57
  127.7 0.1 reshape.45
  127.8 6.4 %all-to-all-done.3 = bf16[32,8,384]{2,0,1:T(8,128)(2,1)S(1)} async-done(((bf16[32,8,384]{2,0,1:T(8,128)(2,1)}), bf16[32,8,384]{2,0,1:T(8,128)(2,1)S(1)}, u32[]{:S(2)}, u32[]{:S(2)}) %all-to-all-start.3) | async-done | bytes 196640 | tf_op jit(solution)/shard_map/all_to_all | solution.py:14
  134.2 0.1 reshape.48
  134.2 1.2 fusion.33
  135.5 0.1 fusion.19
  135.6 0.0 all-gather.3.cloned.1.call-done
  135.6 4.7 %copy.46 = bf16[4096,384]{0,1:T(8,128)(2,1)} copy(bf16[4096,384]{1,0:T(8,128)(2,1)} %all-gather.3.cloned.1.call-done) | data formatting | bytes 6291456 | tf_op jit(solution)/shard_map/all_gather | solution.py:24
  140.4 3.8 %multiply_reduce_fusion = (f32[3,256]{1,0:T(4,128)S(1)}, f32[3,256,4096]{2,1,0:T(8,128)S(1)}) fusion(bf16[4096,3,128]{0,2,1:T(8,128)(2,1)} %bitcast.61, bf16[256,3,128]{2,1,0:T(4,128)(2,1)S(1)} %reshape.45), kind=kOutput, calls=%fused_computation.1 | convolution fusion | flops 811597056 | bytes 15928320 | tf_op jit(solution)/shard_map/rhd,nhd->hrn/dot_general | solution.py:30
  144.2 0.0 copy-start.1
  144.2 4.5 %copy-done.1 = f32[3,256,4096]{2,1,0:T(8,128)} copy-done((f32[3,256,4096]{2,1,0:T(8,128)}, f32[3,256,4096]{2,1,0:T(8,128)S(1)}, u32[]{:S(2)}) %copy-start.1) | copy-done | bytes 12582936
  148.7 2.2 %fusion = f32[3,256]{1,0:T(4,128)S(1)} fusion(f32[3,256,4096]{2,1,0:T(8,128)S(1)} %get-tuple-element.8, f32[3,256]{1,0:T(4,128)S(1)} %get-tuple-element.7), kind=kLoop, calls=%fused_computation.2 | loop fusion | flops 9436416 | bytes 12589056 | tf_op jit(solution)/shard_map/reduce_sum | solution.py:36
  150.9 0.0 copy-start.2
  151.0 27.9 %all-gather.5.cloned.1.call-done = bf16[4096,384]{1,0:T(8,128)(2,1)} async-done(((bf16[256,384]{1,0:T(8,128)(2,1)}), bf16[4096,384]{1,0:T(8,128)(2,1)}) %all-gather.5.cloned.1.call-update) | async-done | bytes 3145744 | tf_op jit(solution)/shard_map/all_gather | solution.py:25
  178.8 4.7 %copy.50 = bf16[4096,384]{0,1:T(8,128)(2,1)} copy(bf16[4096,384]{1,0:T(8,128)(2,1)} %all-gather.5.cloned.1.call-done) | data formatting | bytes 6291456 | tf_op jit(solution)/shard_map/all_gather | solution.py:25
  183.5 6.9 %fusion.16 = f32[256,3,128]{2,0,1:T(8,128)S(1)} fusion(bf16[4096,3,128]{0,2,1:T(8,128)(2,1)} %bitcast.62, f32[3,256,4096]{2,1,0:T(8,128)} %copy-done.1, f32[3,256]{1,0:T(4,128)S(1)} %get-tuple-element.7, f32[256,3]{0,1:T(4,128)S(1)} %bitcast_add_fusion, f32[256,3]{0,1:T(4,128)S(1)} %multiply_bitcast_fusion), kind=kOutput, calls=%fused_computation.15 | convolution fusion | flops 814940160 | bytes 16131072 | tf_op jit(solution)/shard_map/hrn,nhd->hrd/dot_general | solution.py:37
  190.4 0.0 copy-done.2
  190.4 0.4 fusion.15
  190.8 0.2 copy.60
  191.0 0.2 convert_element_type.20
  191.2 14.6 %all_to_all.88 = bf16[8,32,384]{2,1,0:T(8,128)(2,1)S(1)} all-to-all(bf16[8,32,384]{2,1,0:T(8,128)(2,1)S(1)} %convert_element_type.20), channel_id=1, replica_groups=mesh['blk'=16,'uly'=8,'clip'=4] {'uly'}, dimensions={0} | all-to-all | bytes 393216 | tf_op jit(solution)/shard_map/all_to_all | solution.py:74
  205.7 0.7 copy.71
  (3 shorter events, 0.1 us)
Async XLA Ops:
  6.5 33.4 %copy-start = (bf16[256,4096]{1,0:T(8,128)(2,1)S(1)}, bf16[256,4096]{1,0:T(8,128)(2,1)}, u32[]{:S(2)}) copy-start(bf16[256,4096]{1,0:T(8,128)(2,1)} %param.10) | copy-start | bytes 6291460
  6.5 129.1 %all-gather.3.cloned.1.call-start = ((), (), s32[]{:S(2)}) async-start(), calls=%async_computation.5 | async-start | bytes 3342336 | tf_op jit(solution)/shard_map/all_gather | solution.py:24
  22.7 156.2 %all-gather.5.cloned.1.call-start = ((), (), s32[]{:S(2)}) async-start(), calls=%async_computation.6 | async-start | bytes 3342336 | tf_op jit(solution)/shard_map/all_gather | solution.py:25
  36.6 82.5 %all-to-all-start = ((bf16[32,8,384]{2,0,1:T(8,128)(2,1)}), bf16[32,8,384]{2,0,1:T(8,128)(2,1)S(1)}, u32[]{:S(2)}, u32[]{:S(2)}) async-start(bf16[32,8,384]{2,0,1:T(8,128)(2,1)} %bitcast.60), calls=%async_computation | async-start | bytes 393216 | tf_op jit(solution)/shard_map/all_to_all | solution.py:11
  119.0 15.1 %all-to-all-start.3 = ((bf16[32,8,384]{2,0,1:T(8,128)(2,1)}), bf16[32,8,384]{2,0,1:T(8,128)(2,1)S(1)}, u32[]{:S(2)}, u32[]{:S(2)}) async-start(bf16[32,8,384]{2,0,1:T(8,128)(2,1)} %bitcast.57), calls=%async_computation.3 | async-start | bytes 393216 | tf_op jit(solution)/shard_map/all_to_all | solution.py:14
  144.2 4.6 %copy-start.1 = (f32[3,256,4096]{2,1,0:T(8,128)}, f32[3,256,4096]{2,1,0:T(8,128)S(1)}, u32[]{:S(2)}) copy-start(f32[3,256,4096]{2,1,0:T(8,128)S(1)} %get-tuple-element.8) | copy-start | bytes 37748740
  150.9 39.5 %copy-start.2 = (bf16[256,1,384]{0,2,1:T(8,128)(2,1)S(1)}, bf16[256,1,384]{0,2,1:T(8,128)(2,1)}, u32[]{:S(2)}) copy-start(bf16[256,1,384]{0,2,1:T(8,128)(2,1)} %copy.57) | copy-start | bytes 589828
Sparse Core Ops, SparseCore 0:
  22.8 79.6 all-gather.2
  104.6 74.1 all-gather.4
where the time goes:
time: 214 us; the launch traced here: 213 us
  blocking collectives  117 us (55%)
  waiting for transfers between devices  34.4 us (16%)
  local copies, waits for them, and re-layouts  22.1 us (10%)
  matrix products  13.6 us (6%)
  between operations  13.5 us (6%)
  starting transfers between devices  10.4 us (5%)
  other arithmetic  2.33 us (1%)
    psum x1, blocking collectives, on_device(): lax.psum(jnp.einsum('rc,cjk->rjk', columns, text_projection, preferred_el...  76.2 us
    all_gather x1, waiting for transfers between devices, on_device(): value_block = lax.all_gather(local_value, 'blk', axis=0, tiled=True)  27.9 us
    all_to_all x1, blocking collectives, on_device(): lax.all_to_all(self_keys, 'uly', split_axis=1, concat_axis=0, tiled=True)  15 us
    all_to_all x1, blocking collectives, on_device(): lax.all_to_all(combined, 'uly', split_axis=0, concat_axis=1, tiled=True)  14.6 us
    all_to_all x1, blocking collectives, on_device(): lax.all_to_all(self_values, 'uly', split_axis=1, concat_axis=0, tiled=True)  11.2 us
    all_to_all x1, starting transfers between devices, on_device(): lax.all_to_all(cross_queries, 'uly', split_axis=1, concat_axis=0, tiled=T...  6.95 us
    dot_general x1, matrix products, on_device(): jnp.einsum('hrn,nhd->hrd', weights.astype(jnp.bfloat16), value_heads, pre...  6.91 us
    all_to_all x1, waiting for transfers between devices, on_device(): lax.all_to_all(cross_queries, 'uly', split_axis=1, concat_axis=0, tiled=T...  6.42 us
  transfers between devices with their start and end apart: 4, of which 2 were waited for; matrix products, arithmetic and copies ran while one was open for 9% of the time, Pallas kernels for 0%

commit v1 on v0

v1 whole, which is shorter than its diff:
```python
import math

import jax
import jax.numpy as jnp
from jax import lax
from jax.experimental import pallas as pl
from jax.experimental.pallas import tpu as pltpu
from jax.sharding import PartitionSpec as P

HEADS = 24
HEAD_DIM = 128
NX, NY, NZ = 4, 2, 16
SOURCES = NY * NZ
GROUPS = NX * NY
ROWS = 32
HALF = ROWS // 2
GROUP_COLS = HEADS // GROUPS * HEAD_DIM
TEXT_ROWS = 256
CHUNK = TEXT_ROWS // NZ
FEATURES = 256
TILE = 256
TILE_SOURCES = TILE // HALF
EXP_SCALE = math.log2(math.e) / math.sqrt(HEAD_DIM)
F32, BF16 = jnp.float32, jnp.bfloat16


def remote(src, dst, send_sem, recv_sem, device):
    return pltpu.make_async_remote_copy(
        src_ref=src,
        dst_ref=dst,
        send_sem=send_sem,
        recv_sem=recv_sem,
        device_id=device,
        device_id_type=pl.DeviceIdType.MESH,
    )


def drain(ref, sem):
    pltpu.make_async_copy(ref, ref, sem).wait()


def slot_of(head):
    pair, place = head // 3, head % 3
    z = 2 * pair + jnp.where(place == 2, 1, 0)
    y = jnp.where(place == 2, pair % 2, place)
    return z, y


def scores_of(queries, keys):
    return lax.dot_general(queries, keys, (((1,), (1,)), ((), ())), preferred_element_type=F32)


def attend(queries, blocks):
    top = total = acc = None
    for keys, values in blocks:
        scores = scores_of(queries, keys())
        block_top = jnp.max(scores, axis=1, keepdims=True)
        new_top = block_top if top is None else jnp.maximum(top, block_top)
        weights = jnp.exp2((scores - new_top) * EXP_SCALE)
        block_total = jnp.sum(weights, axis=1, keepdims=True)
        update = jnp.dot(weights.astype(BF16), values(), preferred_element_type=F32)
        if top is None:
            total, acc = block_total, update
        else:
            shrink = jnp.exp2((top - new_top) * EXP_SCALE)
            total = total * shrink + block_total
            acc = acc * shrink + update
        top = new_top
    return acc / total


def kernel(
    q_hbm, k_hbm, v_hbm, cq_hbm, text_hbm, proj_hbm, out_ref,
    q_in, k_in, v_in, cq_in, text_in, proj_in,
    kv_stage, kv, q_got, o_stage, o_got,
    cq_got, co_stage, co_got,
    part, up_got, down_got, text_kv,
    load_sem, kv_send, kv_recv, q_send, q_recv, x_send, x_recv, cross_send, cross_recv,
    rs_send, rs_recv, ag_send, ag_recv, o_send, o_recv,
):
    z, uly, clip = lax.axis_index("blk"), lax.axis_index("uly"), lax.axis_index("clip")
    x, y = uly // NY, uly % NY
    me = z * NY + y
    active = jnp.logical_or(z % 2 == 0, y == (z // 2) % 2)
    my_head = 3 * (z // 2) + jnp.where(z % 2 == 0, y, 2)
    first_head = 3 * (z // 2) + 2 * (z % 2)

    def device(to_z, to_x, to_y):
        return (to_z, to_x * NY + to_y, clip)

    barrier = pltpu.get_barrier_semaphore()

    @pl.loop(1, SOURCES)
    def _(k):
        s = lax.rem(me + k, SOURCES)
        pl.semaphore_signal(
            barrier, inc=1, device_id=device(s // NY, x, s % NY), device_id_type=pl.DeviceIdType.MESH
        )

    @pl.loop(0, NY * (NX - 1))
    def _(k):
        to_x = lax.rem(x + 1 + k // NY, NX)
        pl.semaphore_signal(
            barrier, inc=1, device_id=device(z, to_x, k % NY), device_id_type=pl.DeviceIdType.MESH
        )

    loads = [
        pltpu.make_async_copy(k_hbm, k_in, load_sem.at[0]),
        pltpu.make_async_copy(v_hbm, v_in, load_sem.at[1]),
        pltpu.make_async_copy(
            text_hbm.at[:, pl.ds(pl.multiple_of(z * FEATURES, FEATURES), FEATURES)], text_in, load_sem.at[2]
        ),
        pltpu.make_async_copy(proj_hbm, proj_in, load_sem.at[3]),
        pltpu.make_async_copy(cq_hbm, cq_in, load_sem.at[4]),
        pltpu.make_async_copy(q_hbm, q_in, load_sem.at[5]),
    ]
    for load in loads:
        load.start()
    loads[0].wait()
    loads[1].wait()
    for h in range(HEADS):
        cols = slice(h * HEAD_DIM, (h + 1) * HEAD_DIM)
        for g in range(2):
            rows = slice(g * HALF, (g + 1) * HALF)
            kv_stage[g, h, 0] = k_in[rows, cols]
            kv_stage[g, h, 1] = v_in[rows, cols]
    loads[2].wait()
    loads[3].wait()
    part[...] = jnp.dot(text_in[...], proj_in[...], preferred_element_type=F32).reshape(part.shape)
    loads[4].wait()
    loads[5].wait()

    pl.semaphore_wait(barrier, SOURCES - 1 + NY * (NX - 1))

    def send_heads(source, target, send_sem, recv_sem):
        @pl.loop(0, HEADS)
        def _(k):
            h = lax.rem(first_head + k, HEADS)
            to_z, to_y = slot_of(h)
            mine = jnp.logical_and(to_z == z, to_y == y)

            @pl.when(mine)
            def _():
                pltpu.make_async_copy(source(h), target, recv_sem).start()

            @pl.when(jnp.logical_not(mine))
            def _():
                remote(source(h), target, send_sem, recv_sem, device(to_z, x, to_y)).start()

    def send_kv(g):
        send_heads(lambda h: kv_stage.at[g, h], kv.at[x, g, me], kv_send.at[g], kv_recv.at[g])

    def send_q(g):
        def source(h):
            return q_in.at[pl.ds(g * HALF, HALF), pl.ds(pl.multiple_of(h * HEAD_DIM, HEAD_DIM), HEAD_DIM)]

        send_heads(source, q_got.at[g, me], q_send.at[g], q_recv.at[g])

    def to_groups(source, target, send_sem, recv_sem):
        @pl.loop(1, GROUPS)
        def _(k):
            to = lax.rem(uly + k, GROUPS)
            remote(source(to), target, send_sem, recv_sem, device(z, to // NY, to % NY)).start()

        pltpu.make_async_copy(source(uly), target, recv_sem).start()

    def x_copy(g, j):
        step = (1, 3, 2)[j]
        return remote(
            kv.at[x, g], kv.at[x, g], x_send.at[g, j], x_recv.at[g, j], device(z, lax.rem(x + step, NX), y)
        )

    def gather_x(g):
        @pl.when(active)
        def _():
            drain(kv.at[x, g], kv_recv.at[g])
            for j in range(3):
                x_copy(g, j).start()

    above, below = lax.rem(z + 1, NZ), lax.rem(z + NZ - 1, NZ)

    def rs_up(i):
        chunk = lax.rem(z + NZ // 2 - i + NZ, NZ)
        return chunk, remote(part.at[chunk], up_got.at[i], rs_send.at[0, i], rs_recv.at[0, i], device(above, x, y))

    def rs_down(i):
        chunk = lax.rem(z - (NZ // 2 - 1) + i + NZ, NZ)
        return chunk, remote(part.at[chunk], down_got.at[i], rs_send.at[1, i], rs_recv.at[1, i], device(below, x, y))

    def ag_up(i):
        chunk = lax.rem(z - i + NZ, NZ)
        return remote(text_kv.at[chunk], text_kv.at[chunk], ag_send.at[0, i], ag_recv.at[0, i], device(above, x, y))

    def ag_down(i):
        chunk = lax.rem(z + i, NZ)
        return remote(text_kv.at[chunk], text_kv.at[chunk], ag_send.at[1, i], ag_recv.at[1, i], device(below, x, y))

    def rs_step(i):
        chunk, copy = rs_up(i)
        if i:
            rs_up(i - 1)[1].wait_recv()
            part[chunk] = part[chunk] + up_got[i - 1]
        copy.start()
        if i < NZ // 2 - 1:
            chunk, copy = rs_down(i)
            if i:
                rs_down(i - 1)[1].wait_recv()
                part[chunk] = part[chunk] + down_got[i - 1]
            copy.start()

    def ag_step(i):
        if i:
            ag_up(i - 1).wait_recv()
        ag_up(i).start()
        if i < NZ // 2 - 1:
            if i:
                ag_down(i - 1).wait_recv()
            ag_down(i).start()

    steps = NZ // 2
    rs_step(0)
    send_kv(0)
    to_groups(
        lambda to: cq_in.at[:, pl.ds(pl.multiple_of(to * GROUP_COLS, HEAD_DIM), GROUP_COLS)],
        cq_got.at[uly],
        cross_send.at[0],
        cross_recv.at[0],
    )
    rs_step(1)
    send_kv(1)
    rs_step(2)
    rs_step(3)
    send_q(0)
    rs_step(4)
    gather_x(0)
    rs_step(5)
    send_q(1)
    rs_step(6)
    rs_step(7)
    rs_up(steps - 1)[1].wait_recv()
    rs_down(steps - 2)[1].wait_recv()
    text_kv[z] = (part[z] + up_got[steps - 1] + down_got[steps - 2]).astype(BF16)
    ag_step(0)
    gather_x(1)
    for i in range(1, steps):
        ag_step(i)
    ag_up(steps - 1).wait_recv()
    ag_down(steps - 2).wait_recv()
    drain(cq_got, cross_recv.at[0])
    for j in range(GROUP_COLS // HEAD_DIM):
        cols = slice(j * HEAD_DIM, (j + 1) * HEAD_DIM)
        vcols = slice(GROUP_COLS + j * HEAD_DIM, GROUP_COLS + (j + 1) * HEAD_DIM)
        queries = cq_got[:, :, cols].reshape(GROUPS * ROWS, HEAD_DIM)
        keys = text_kv[:, :, cols].reshape(TEXT_ROWS, HEAD_DIM)
        values = text_kv[:, :, vcols].reshape(TEXT_ROWS, HEAD_DIM)
        result = attend(queries, [(lambda: keys, lambda: values)])
        co_stage[:, :, cols] = result.astype(BF16).reshape(GROUPS, ROWS, HEAD_DIM)
    to_groups(lambda to: co_stage.at[to], co_got.at[uly], cross_send.at[1], cross_recv.at[1])

    @pl.when(active)
    def _():
        for g in range(2):
            for j in range(3):
                x_copy(g, j).wait_recv()

        def block(step):
            at = lax.rem(x + step, NX)
            rows = 2 * SOURCES * HALF
            return (
                lambda: kv[at, :, :, 0].reshape(rows, HEAD_DIM),
                lambda: kv[at, :, :, 1].reshape(rows, HEAD_DIM),
            )

        for g in range(2):
            drain(q_got.at[g], q_recv.at[g])

            @pl.loop(0, SOURCES // TILE_SOURCES)
            def _(t):
                here = pl.ds(t * TILE_SOURCES, TILE_SOURCES)
                queries = q_got[g, here].reshape(TILE, HEAD_DIM)
                result = attend(queries, [block(step) for step in range(NX)])
                o_stage[g, here] = result.astype(BF16).reshape(TILE_SOURCES, HALF, HEAD_DIM)

                @pl.loop(0, TILE_SOURCES)
                def _(k):
                    s = t * TILE_SOURCES + k
                    target = o_got.at[my_head, pl.ds(g * HALF, HALF)]

                    @pl.when(s == me)
                    def _():
                        pltpu.make_async_copy(o_stage.at[g, s], target, o_recv.at[g]).start()

                    @pl.when(s != me)
                    def _():
                        remote(
                            o_stage.at[g, s], target, o_send.at[g], o_recv.at[g], device(s // NY, x, s % NY)
                        ).start()

    drain(co_got, cross_recv.at[1])
    for g in range(2):
        drain(o_got.at[:, pl.ds(g * HALF, HALF)], o_recv.at[g])
        rows = slice(g * HALF, (g + 1) * HALF)
        for h in range(HEADS):
            per = GROUP_COLS // HEAD_DIM
            cross = co_got[h // per, rows, (h % per) * HEAD_DIM : (h % per + 1) * HEAD_DIM]
            total = o_got[h, rows].astype(F32) + cross.astype(F32)
            out_ref[rows, h * HEAD_DIM : (h + 1) * HEAD_DIM] = total.astype(BF16)

    for i in range(steps):
        rs_up(i)[1].wait_send()
        ag_up(i).wait_send()
    for i in range(steps - 1):
        rs_down(i)[1].wait_send()
        ag_down(i).wait_send()
    drain(cq_got.at[pl.ds(0, GROUPS - 1)], cross_send.at[0])
    drain(co_got.at[pl.ds(0, GROUPS - 1)], cross_send.at[1])

    @pl.when(active)
    def _():
        for g in range(2):
            drain(kv_stage.at[g, pl.ds(0, HEADS - 1)], kv_send.at[g])
            drain(q_got.at[g, pl.ds(0, HEADS - 1)], q_send.at[g])
            drain(o_stage.at[g, pl.ds(0, SOURCES - 1)], o_send.at[g])
            for j in range(3):
                x_copy(g, j).wait_send()

    @pl.when(jnp.logical_not(active))
    def _():
        for g in range(2):
            drain(kv_stage.at[g], kv_send.at[g])
            drain(q_got.at[g, pl.ds(0, HEADS)], q_send.at[g])


def on_device(self_queries, self_keys, self_values, cross_queries, text_rows, text_projection):
    projection = text_projection.reshape(FEATURES, 2 * GROUP_COLS)
    any_space = pl.BlockSpec(memory_space=pl.ANY)
    dma = pltpu.SemaphoreType.DMA
    tokens = (ROWS, HEADS * HEAD_DIM)
    return pl.pallas_call(
        kernel,
        out_shape=jax.ShapeDtypeStruct(tokens, BF16),
        in_specs=[any_space] * 6,
        out_specs=pl.BlockSpec(memory_space=pltpu.VMEM),
        scratch_shapes=[
            pltpu.VMEM(tokens, BF16),
            pltpu.VMEM(tokens, BF16),
            pltpu.VMEM(tokens, BF16),
            pltpu.VMEM(tokens, BF16),
            pltpu.VMEM((TEXT_ROWS, FEATURES), BF16),
            pltpu.VMEM((FEATURES, 2 * GROUP_COLS), BF16),
            pltpu.VMEM((2, HEADS, 2, HALF, HEAD_DIM), BF16),
            pltpu.VMEM((NX, 2, SOURCES, 2, HALF, HEAD_DIM), BF16),
            pltpu.VMEM((2, SOURCES, HALF, HEAD_DIM), BF16),
            pltpu.VMEM((2, SOURCES, HALF, HEAD_DIM), BF16),
            pltpu.VMEM((HEADS, ROWS, HEAD_DIM), BF16),
            pltpu.VMEM((GROUPS, ROWS, GROUP_COLS), BF16),
            pltpu.VMEM((GROUPS, ROWS, GROUP_COLS), BF16),
            pltpu.VMEM((GROUPS, ROWS, GROUP_COLS), BF16),
            pltpu.VMEM((NZ, CHUNK, 2 * GROUP_COLS), F32),
            pltpu.VMEM((NZ // 2, CHUNK, 2 * GROUP_COLS), F32),
            pltpu.VMEM((NZ // 2 - 1, CHUNK, 2 * GROUP_COLS), F32),
            pltpu.VMEM((NZ, CHUNK, 2 * GROUP_COLS), BF16),
            dma((6,)),
            dma((2,)), dma((2,)),
            dma((2,)), dma((2,)),
            dma((2, 3)), dma((2, 3)),
            dma((2,)), dma((2,)),
            dma((2, NZ // 2)), dma((2, NZ // 2)),
            dma((2, NZ // 2)), dma((2, NZ // 2)),
            dma((2,)), dma((2,)),
        ],
        compiler_params=pltpu.CompilerParams(
            collective_id=0, has_side_effects=True, vmem_limit_bytes=48 * 2**20
        ),
    )(self_queries, self_keys, self_values, cross_queries, text_rows, projection)


def solution(mesh):
    tokens = P(("clip", "blk", "uly"), None)
    return jax.shard_map(
        on_device,
        mesh=mesh,
        in_specs=(tokens, tokens, tokens, tokens, P("clip", None), P("blk", None, "uly")),
        out_specs=tokens,
        check_vma=False,
    )
```

time: 214 us -> 108 us (0.50)
  the two profiles are of different devices: /device:TPU:32 before, /device:TPU:2 now
where the time goes in v1:
time: 108 us
  Pallas kernels  100 us (93%)
  local copies, waits for them, and re-layouts  7.02 us (6%)
    pallas_call x1, Pallas kernels, on_device(): pl.pallas_call(kernel, out_shape=jax.ShapeDtypeStruct(tokens, BF16), in_s...  100 us
    unnamed x12, local copies, waits for them, and re-layouts  7.02 us

profile of v1, /device:TPU:2, one launch (start us, length us, event | category | flops | bytes accessed | tf_op | source)
XLA Modules:
  0.0 107.5 jit_solution(946596466027035493)
XLA Ops:
  0.0 1.0 copy.7
  1.0 0.0 copy-start
  1.1 1.6 %copy-done = bf16[256,4096]{1,0:T(8,128)(2,1)S(1)} copy-done((bf16[256,4096]{1,0:T(8,128)(2,1)S(1)}, bf16[256,4096]{1,0:T(8,128)(2,1)}, u32[]{:S(2)}) %copy-start) | copy-done | bytes 2097176
  2.6 0.0 copy-start.1
  2.6 0.9 copy-done.1
  3.6 0.0 copy-start.2
  3.6 0.9 copy-done.2
  4.5 0.0 copy-start.3
  4.5 0.9 copy-done.3
  5.4 0.0 copy-start.4
  5.4 0.9 copy-done.4
  6.4 100.5 %shard_map.64 = bf16[32,3072]{1,0:T(8,128)(2,1)S(1)} custom-call(bf16[32,3072]{1,0:T(8,128)(2,1)S(1)} %copy-done.1, bf16[32,3072]{1,0:T(8,128)(2,1)S(1)} %copy-done.2, bf16[32,3072]{1,0:T(8,128)(2,1)S(1)} %copy-done.3, bf16[32,3072]{1,0:T(8,128)(2,1)S(1)} %copy-done.4, bf16[256,4096]{1,0:T(8,128)(2,1)S(1)} %copy-done, bf16[256,768]{1,0:T(8,128)(2,1)S(1)} %bitcast.2), custom_call_target="tpu_custom_call" | custom-call | tf_op jit(solution)/shard_map/pallas_call | solution.py:339
  106.8 0.7 copy.9
Async XLA Ops:
  1.0 1.6 %copy-start = (bf16[256,4096]{1,0:T(8,128)(2,1)S(1)}, bf16[256,4096]{1,0:T(8,128)(2,1)}, u32[]{:S(2)}) copy-start(bf16[256,4096]{1,0:T(8,128)(2,1)} %text_hbm.1) | copy-start | bytes 6291460
  2.6 0.9 copy-start.1
  3.6 0.9 copy-start.2
  4.5 0.9 copy-start.3
  5.4 0.9 copy-start.4
